TPU v7x, 256 devices: a whole 4x4x8 slice. The times are simulated.
256 devices in a mesh: ab: 16 (over y_hi, x, core), cd: 16 (over y_lo, z).
Axes of the slice: x: 4, y: 4 (y_hi: 2, y_lo: 2; y = y_hi * 2 + y_lo), z: 8, core: 2. Of those that a mesh axis runs over, the one named last changes fastest.
Arguments:
- amplitudes: float32 [384, 640000], P('cd', 'ab'), may hold values from -6 to 6
- integrals: float32 [800, 640000], P(None, ('ab', 'cd')), may hold values from -0.015625 to 0.015625
- pair_index: int32 [384], P('cd'), may hold values from 0 to 9999
- occ_energy: float32 [100], replicated, may hold values from -2 to -0.3
- virt_energy: float32 [800], replicated, may hold values from 0.2 to 4
Outputs:
- increment: float32 [384, 800], P('cd', 'ab')
All inputs are finite; a program needn't handle non-finite values.
Results may differ from a plain program's by a relative error of at most 0.00012.
Values sent between devices are 32-bit elements; how exact they have to be, the bound alone decides.
A program may use at most 128 MiB of HBM per device.

v0:
```python
import jax
import jax.numpy as jnp
from jax import lax
from jax.sharding import PartitionSpec as P

NOCC = 100
NV = 800


def lookup(table, indices):
    places = jnp.arange(table.shape[0], dtype=jnp.int32)
    onehot = indices[:, None] == places[None, :]
    return jnp.sum(jnp.where(onehot, table[None, :], jnp.float32(0.0)), axis=1)


def per_device(amplitudes, integrals, pair_index, occ_energy, virt_energy):
    pieces = lax.axis_size("cd")
    local_rows = amplitudes.shape[0]
    width_each = amplitudes.shape[1] // pieces
    window = integrals.shape[0]
    blocks = amplitudes.reshape(local_rows, pieces, width_each)
    received = lax.all_to_all(blocks, "cd", split_axis=1, concat_axis=0, tiled=True)
    received = received.reshape(pieces * local_rows, width_each)
    partial_value = lax.dot_general(
        received,
        integrals,
        (((1,), (1,)), ((), ())),
        precision=lax.Precision.HIGHEST,
        preferred_element_type=jnp.float32,
    )
    groups = lax.axis_size("ab")
    window_dev = window // groups
    section_one = lax.psum_scatter(partial_value, "cd", scatter_dimension=0, tiled=True)
    ladder = lax.psum_scatter(section_one, "ab", scatter_dimension=1, tiled=True)
    first_occ = pair_index // NOCC
    second_occ = pair_index % NOCC
    row_ids = lax.axis_index("ab") * window_dev + jnp.arange(window_dev, dtype=jnp.int32)
    outer_virt = row_ids // NV
    inner_virt = row_ids % NV
    occ_pair = lookup(occ_energy, first_occ) + lookup(occ_energy, second_occ)
    virt_pair = lookup(virt_energy, outer_virt) + lookup(virt_energy, inner_virt)
    denominator = occ_pair[:, None] - virt_pair[None, :]
    return ladder / denominator


def solution(mesh):
    return jax.shard_map(
        per_device,
        mesh=mesh,
        in_specs=(P("cd", "ab"), P(None, ("ab", "cd")), P("cd"), P(), P()),
        out_specs=P("cd", "ab"),
        check_vma=False,
    )
```

profile of v0, /device:TPU:1, one launch (start us, length us, event | category | flops | bytes accessed | tf_op | source)
XLA Modules:
  0.0 342.3 jit_solution(8088441555754034571)
XLA Ops:
  6.5 0.0 reduce-scatter.6.cloned.1.call-start
  6.5 6.0 %reshape.39 = f32[24,16,2500]{2,1,0:T(8,128)} reshape(f32[24,40000]{1,0:T(8,128)} %param.5) | data formatting | bytes 7680000 | tf_op jit(solution)/shard_map/reshape | solution.py:21
  12.5 4.5 %copy.8 = f32[24,16,2500]{2,0,1:T(8,128)S(1)} copy(f32[24,16,2500]{2,1,0:T(8,128)} %reshape.39) | data formatting | bytes 7680000 | tf_op jit(solution)/shard_map/reshape | solution.py:21
  17.1 0.0 slice-start.1
  17.1 97.7 %all_to_all.15 = f32[24,16,2500]{2,0,1:T(8,128)S(1)} all-to-all(f32[24,16,2500]{2,0,1:T(8,128)S(1)} %copy.8), channel_id=1, replica_groups=mesh['ab'=16,'cd'=16] {'cd'}, dimensions={1} | all-to-all | bytes 7680000 | tf_op jit(solution)/shard_map/all_to_all | solution.py:22
  114.8 0.0 slice-done
  114.8 0.0 slice-done.1
  114.8 0.0 copy-start
  114.8 0.0 copy-start.2
  114.8 0.0 copy-start.1
  114.9 14.0 %fusion.1 = f32[384,800]{1,0:T(8,128)} fusion(f32[384,2500]{1,0:T(8,128)S(1)} %bitcast.11, f32[800,2500]{1,0:T(8,128)S(1)} %bitcast.13), kind=kOutput, calls=%fused_computation.15 | convolution fusion | flops 9216000000 | bytes 13068800 | tf_op jit(solution)/shard_map/dot_general | solution.py:24
  128.8 0.0 reduce-scatter.6.cloned.1.call-update
  128.8 0.0 all-reduce.4.cloned.1.call-start
  128.9 0.0 copy-done.3
  128.9 0.6 dynamic-slice.2
  130.2 0.0 copy-done
  130.2 0.2 select_reduce_fusion
  130.4 0.0 copy-done.2
  130.4 60.0 %reduce-scatter.6.cloned.1.call-done = f32[24,800]{1,0:T(8,128)} async-done(((f32[384,800]{1,0:T(8,128)}), f32[24,800]{1,0:T(8,128)}) %reduce-scatter.6.cloned.1.call-update) | async-done | bytes 76816
  190.4 0.0 all-reduce.4.cloned.1.call-update
  190.4 0.0 copy-done.1
  190.5 0.2 select_reduce_fusion.2
  190.6 143.4 %all-reduce.4.cloned.1.call-done = f32[24,800]{1,0:T(8,128)} async-done(((f32[24,800]{1,0:T(8,128)}), f32[24,800]{1,0:T(8,128)}) %all-reduce.4.cloned.1.call-update) | async-done | bytes 76816
  334.0 1.4 dynamic-slice_divide_fusion
  (7 shorter events, 0.0 us)
Async XLA Ops:
  6.5 183.9 %reduce-scatter.6.cloned.1.call-start = ((), (), s32[]{:S(2)}) async-start(), calls=%async_computation.3 | async-start | bytes 1462272
  12.5 102.3 %slice-start = ((s8[8192000]{0:T(1024)(128)(4,1)}), s8[4194304]{0:T(1024)(128)(4,1)S(1)}, s32[]{:S(2)}) async-start(s8[8192000]{0:T(1024)(128)(4,1)} %bitcast.12), calls=%async_computation.4 | async-start | bytes 8388608
  17.1 97.7 %slice-start.1 = ((s8[8192000]{0:T(1024)(128)(4,1)}), s8[3997696]{0:T(1024)(128)(4,1)S(1)}, s32[]{:S(2)}) async-start(s8[8192000]{0:T(1024)(128)(4,1)} %bitcast.12), calls=%async_computation.5 | async-start | bytes 7995392
  114.8 14.1 %copy-start.3 = (u32[256]{0:T(256)S(1)}, u32[256]{0:T(256)}, u32[]{:S(2)}) copy-start(u32[256]{0:T(256)} %constant.55) | copy-start | bytes 3076
  114.8 15.4 %copy-start = (f32[800]{0:T(1024)S(1)}, f32[800]{0:T(1024)}, u32[]{:S(2)}) copy-start(f32[800]{0:T(1024)} %param.9) | copy-start | bytes 9604
  114.8 15.6 %copy-start.2 = (s32[24]{0:T(128)S(1)}, s32[24]{0:T(128)}, u32[]{:S(2)}) copy-start(s32[24]{0:T(128)} %param.7) | copy-start | bytes 292
  114.8 75.6 %copy-start.1 = (f32[100]{0:T(128)S(1)}, f32[100]{0:T(128)}, u32[]{:S(2)}) copy-start(f32[100]{0:T(128)} %param.8) | copy-start | bytes 1204
  128.8 205.2 %all-reduce.4.cloned.1.call-start = ((), (), s32[]{:S(2)}) async-start(), calls=%async_computation.2 | async-start | bytes 172032
Sparse Core Ops, SparseCore 0:
  129.0 61.4 reduce-scatter.5
  193.0 140.9 all-reduce.3
where the time goes:
time: 343 us; the launch traced here: 342 us
  waiting for transfers between devices  203 us (59%)
  blocking collectives  97.7 us (28%)
  between operations  14.2 us (4%)
  matrix products  14 us (4%)
  local copies, waits for them, and re-layouts  11.2 us (3%)
    unnamed x4, waiting for transfers between devices  203 us
    all_to_all x1, blocking collectives, per_device(): lax.all_to_all(blocks, 'cd', split_axis=1, concat_axis=0, tiled=True)  97.7 us
    dot_general x1, matrix products, per_device(): lax.dot_general(received, integrals, (((1,), (1,)), ((), ())), precision=...  14 us
    reshape x2, local copies, waits for them, and re-layouts, per_device(): blocks = amplitudes.reshape(local_rows, pieces, width_each)  10.5 us
  transfers between devices with their start and end apart: 2, of which 2 were waited for; matrix products, arithmetic and copies ran while one was open for 0% of the time, Pallas kernels for 0%

commit v1 on v0

v1 whole, which is shorter than its diff:
```python
import functools

import jax
import jax.numpy as jnp
from jax import lax
from jax.experimental import pallas as pl
from jax.experimental.pallas import tpu as pltpu
from jax.sharding import PartitionSpec as P

NOCC = 100
NV = 800
MESH = pl.DeviceIdType.MESH

ROWS = 24
EACH = 2500
WIDE = 2560
TILES = WIDE // 128
FULL = EACH // 128
REST = EACH - FULL * 128
SENT = (3 * FULL + 2) * 128
COLS = 40000
WINDOW = 800
MINE = 50
LAG = 3

PLUS = ("A4", "A3", "A2", "A4", "A3", "B3", "A2", "A4", "A3", "B3", "B2", "A4", "B1", "B3", "B2", "A1")
MINUS = ("A3", "A2", "A1", "A3", "B4", "A2", "B3", "B4", "A3", "B3", "B4", "B2", "B3", "B4", "B2", "B1")
YORDER = [("m", 4), ("p", 3), ("m", 3), ("p", 2), ("m", 2), ("p", 1), ("m", 1), ("p", 0)]
BATCHES = {
    2: (("own",), ("m", 2)),
    6: (("p", 6), ("m", 5)),
    8: (("p", 8), ("m", 8)),
    11: (("p", 11), ("y", 7)),
    12: (("p", 12), ("m", 12)),
    13: (("p", 13), ("m", 13)),
    14: (("p", 14), ("m", 14)),
    15: (("p", 15), ("m", 15)),
}
NB = len(BATCHES)


def kernel(
    amp, integrals, pair_ref, occ_ref, virt_ref, out,
    amp_v, int_v, vhi, vlo, pack, ybuf, pbuf, mbuf, lhs, part, crecv, xs, xrecv, cs, crow, den,
    amp_sem, int_sem, ysend, yrecv, psend, precv, msend, mrecv, c_s, c_r, x_s, x_r, d_s, d_r,
):
    ab, cd = lax.axis_index("ab"), lax.axis_index("cd")
    core, x, yh = ab % 2, (ab // 2) % 4, ab // 8
    yl, z = cd // 8, cd % 8

    def on_ab(h, xx, c):
        return ((h * 4 + xx) * 2 + c, cd)

    def on_cd(y, zz):
        return (ab, y * 8 + zz)

    amp_copy = pltpu.make_async_copy(amp, amp_v, amp_sem)
    int_copy = pltpu.make_async_copy(integrals, int_v, int_sem)
    amp_copy.start()

    partner_core = on_ab(yh, x, 1 - core)
    partners_x = [on_ab((yh + k // 4) % 2, (x + k) % 4, core) for k in range(1, 8)]
    partner_yl = on_cd(1 - yl, z)
    others_cd = [on_cd((yl + k // 8) % 2, (z + k) % 8) for k in range(1, 16)]
    greeted = others_cd + [partner_core] + partners_x
    barrier = pltpu.get_barrier_semaphore()
    for device in greeted:
        pl.semaphore_signal(barrier, inc=1, device_id=device, device_id_type=MESH)

    lane = lax.broadcasted_iota(jnp.int32, (ROWS, 128), 1)
    lane8 = lax.broadcasted_iota(jnp.int32, (8, 128), 1)

    def owner_piece(k):
        if k == 15:
            return yl * 8 + z
        if k < 8:
            way, far = YORDER[k]
            step = far if way == "p" else 8 - far
            return (1 - yl) * 8 + (z + step) % 8
        step = k - 7 if k < 12 else 8 - (k - 11)
        return yl * 8 + (z + step) % 8

    def pack_block(k):
        piece = owner_piece(k)
        begin = piece * EACH
        tile = begin // 128
        off = begin - tile * 128
        turn = lax.rem(128 - off, 128)
        tail = jnp.concatenate(
            [amp_v[:, COLS - 64 : COLS], jnp.zeros((ROWS, 64), jnp.float32)], axis=1
        )
        keep = lane < 128 - off

        def rolled(j):
            if j < TILES:
                block = amp_v[:, pl.ds(pl.multiple_of((tile + j) * 128, 128), 128)]
            else:
                at = jnp.minimum(tile + TILES, COLS // 128 - 1)
                block = amp_v[:, pl.ds(pl.multiple_of(at * 128, 128), 128)]
                block = jnp.where(piece == 15, tail, block)
            return pltpu.roll(block, turn, 1)

        now = rolled(0)
        for j in range(FULL):
            later = rolled(j + 1)
            value = jnp.where(keep, now, later)
            for r in range(3):
                pack[k, :, (r * FULL + j) * 128 : (r * FULL + j + 1) * 128] = value[r * 8 : r * 8 + 8]
            now = later
        value = jnp.where(keep, now, rolled(FULL + 1))
        one, two, three = value[0:8], value[8:16], value[16:24]
        pack[k, :, 3 * FULL * 128 : (3 * FULL + 1) * 128] = jnp.where(lane8 < 64, one, pltpu.roll(two, 64, 1))
        over = REST - 64
        rests = jnp.where(lane8 < REST + over, pltpu.roll(one, over, 1), pltpu.roll(two, 2 * over, 1))
        rests = jnp.where(lane8 < REST + 2 * over, rests, 0.0)
        pack[k, :, (3 * FULL + 1) * 128 : SENT] = jnp.where(lane8 < REST, three, rests)

    def last_tile(ref):
        first = ref[:, 3 * FULL * 128 : (3 * FULL + 1) * 128]
        second = ref[:, (3 * FULL + 1) * 128 : SENT]
        over = REST - 64
        one = jnp.where(lane8 < 64, first, pltpu.roll(second, 128 - over, 1))
        two = jnp.where(lane8 < 64, pltpu.roll(first, 64, 1), pltpu.roll(second, 128 - 2 * over, 1))
        return [jnp.where(lane8 < REST, rest, 0.0) for rest in (one, two, second)]

    def remote(src, dst, send, recv, device):
        return pltpu.make_async_remote_copy(
            src_ref=src, dst_ref=dst, send_sem=send, recv_sem=recv, device_id=device, device_id_type=MESH
        )

    ycopies = [remote(pack.at[k], ybuf.at[k], ysend.at[k], yrecv.at[k], partner_yl) for k in range(8)]
    state = {"y_started": 0, "y_waited": 0}
    packed = set()

    def ensure_pack(k):
        if k not in packed:
            packed.add(k)
            pack_block(k)

    def y_start():
        k = state["y_started"]
        if k < 8:
            ensure_pack(k)
            ycopies[k].start()
            state["y_started"] = k + 1

    def y_wait(k):
        while state["y_waited"] <= k:
            ycopies[state["y_waited"]].wait_recv()
            state["y_waited"] += 1
            y_start()

    yrank = {key: k for k, key in enumerate(YORDER)}
    ring, needs, block_info = {}, {}, {("own",): (0, 0), ("y", 7): (1, 0)}
    for way, sequence, step, buf, send, recv in (
        ("p", PLUS, 1, pbuf, psend, precv),
        ("m", MINUS, 7, mbuf, msend, mrecv),
    ):
        device = on_cd(yl, (z + step) % 8)
        last = {}
        for slot, name in enumerate(sequence):
            far = int(name[1])
            if name in last:
                src, need = buf.at[last[name]], None
            elif name[0] == "A":
                k = 7 + far if way == "p" else 11 + far
                src, need = pack.at[k], ("pack", k)
            else:
                k = yrank[(way, far)]
                src, need = ybuf.at[k], ("y", k)
            last[name] = slot
            ring[way, slot] = remote(src, buf.at[slot], send.at[slot], recv.at[slot], device)
            needs[way, slot] = need
            block_info[way, slot] = (0 if name[0] == "A" else 1, (8 - far) % 8 if way == "p" else far)

    def ring_start(way, slot):
        if slot >= 16:
            return
        need = needs[way, slot]
        if need is not None and need[0] == "pack":
            ensure_pack(need[1])
        elif need is not None:
            y_wait(need[1])
        ring[way, slot].start()

    def split_columns(at, width):
        for place in range(0, 1024, 128):
            pieces = []
            for h in (0, 1):
                g = (h * 4 + place // 128 % 4) * 2 + place // 512
                value = int_v[g * MINE : (g + 1) * MINE, pl.ds(at, width)]
                if width < 128:
                    value = jnp.concatenate([value, jnp.zeros((MINE, 128 - width), jnp.float32)], axis=1)
                pieces += [value, jnp.zeros((64 - MINE, 128), jnp.float32)]
            value = jnp.concatenate(pieces, axis=0).T
            high = value.astype(jnp.bfloat16)
            low = (value - high.astype(jnp.float32)).astype(jnp.bfloat16)
            vhi[place // 256, pl.ds(at, 128), place % 256 : place % 256 + 128] = high
            vlo[place // 256, pl.ds(at, 128), place % 256 : place % 256 + 128] = low

    def split_range(first, end):
        def body(j, carry):
            split_columns(pl.multiple_of(j * 128, 128), 128)
            return carry

        lax.fori_loop(first, end, body, 0)

    batches = list(BATCHES.values())

    def block_ref(block):
        if block[0] == "own":
            return pack.at[15]
        if block[0] == "y":
            return ybuf.at[block[1]]
        return (pbuf if block[0] == "p" else mbuf).at[block[1]]

    core_copies = [remote(part.at[b, 1 - core], crecv.at[b], c_s.at[b], c_r.at[b], partner_core) for b in range(NB)]
    x_copies = [
        [
            remote(
                xs.at[b, (yh + k // 4) % 2 * 4 + (x + k) % 4],
                xrecv.at[b, k - 1], x_s.at[b, k - 1], x_r.at[b, k - 1], partners_x[k - 1],
            )
            for k in range(1, 8)
        ]
        for b in range(NB)
    ]
    owner_copies = {}
    for b in range(NB):
        for i, block in enumerate(batches[b]):
            if block[0] != "own":
                dy, dz = block_info[block]
                device = on_cd((yl + dy) % 2, (z + dz) % 8)
                n = b * 2 + i
                owner_copies[n] = remote(cs.at[n], crow.at[n], d_s.at[n], d_r.at[n], device)

    def multiply(b):
        one, two = (block_ref(block) for block in batches[b])

        def put(value, at, width):
            high = value.astype(jnp.bfloat16)
            lhs[0:48, at : at + width] = high
            lhs[48:96, at : at + width] = (value - high.astype(jnp.float32)).astype(jnp.bfloat16)

        for j in range(0, FULL * 128, 512):
            width = min(512, FULL * 128 - j)
            starts = [r * FULL * 128 + j for r in range(3)]
            put(jnp.concatenate([ref[:, at : at + width] for ref in (one, two) for at in starts], axis=0), j, width)
        put(jnp.concatenate(last_tile(one) + last_tile(two), axis=0), FULL * 128, 128)
        dims = (((1,), (0,)), ((), ()))
        for n in range(4):
            first = lax.dot_general(lhs[...], vhi[n], dims, preferred_element_type=jnp.float32)
            second = lax.dot_general(lhs[0:48, :], vlo[n], dims, preferred_element_type=jnp.float32)
            total = first[0:48] + first[48:96] + second
            part[b, n // 2, :, (n % 2) * 256 : (n % 2) * 256 + 256] = total

    def stage_one(b):
        multiply(b)
        core_copies[b].start()

    def stage_two(b):
        core_copies[b].wait_recv()
        for k in range(4):
            value = part[b, core, :, k * 128 : (k + 1) * 128] + crecv[b, :, k * 128 : (k + 1) * 128]
            turned = pltpu.roll(value, 64, 1)
            xs[b, k] = jnp.where(lane < 64, value[0:ROWS], turned[ROWS:])
            xs[b, 4 + k] = jnp.where(lane < 64, turned[0:ROWS], value[ROWS:])
        for copy in x_copies[b]:
            copy.start()

    def stage_three(b):
        value = xs[b, yh * 4 + x]
        for k, copy in enumerate(x_copies[b]):
            copy.wait_recv()
            value = value + xrecv[b, k]
        turned = pltpu.roll(value, 64, 1)
        for i, block in enumerate(batches[b]):
            n = b * 2 + i
            low, high = (value, turned) if i == 0 else (turned, value)
            high = jnp.concatenate([high[16:24], jnp.zeros((8, 128), jnp.float32)], axis=0)
            both = jnp.where(lane[0:16] < 64, low[0:16], high)
            if block[0] == "own":
                crow[n] = both
            else:
                cs[n] = both
                owner_copies[n].start()

    pl.semaphore_wait(barrier, len(greeted))
    amp_copy.wait()
    int_copy.start()

    y_start()
    for slot in range(LAG):
        ring_start("p", slot)
        ring_start("m", slot)
    y_start()
    for k in range(16):
        ensure_pack(k)

    row24 = lax.broadcasted_iota(jnp.int32, (ROWS, 128), 0)
    occ_pair = jnp.zeros((ROWS, 128), jnp.float32)
    for r in range(ROWS):
        pair = pair_ref[r]
        occ_pair = jnp.where(row24 == r, occ_ref[pair // NOCC] + occ_ref[pair % NOCC], occ_pair)
    virt_pair = jnp.zeros((ROWS, 128), jnp.float32)
    for c in range(MINE):
        row = ab * MINE + c
        virt_pair = jnp.where(lane == c, virt_ref[row // NV] + virt_ref[row % NV], virt_pair)
    den[...] = occ_pair - virt_pair

    int_copy.wait()
    split_columns(FULL * 128, REST)
    splits = {0: (0, 9), 1: (9, 19)}

    for slot in range(16):
        for way in ("p", "m"):
            ring[way, slot].wait_recv()
            ring_start(way, slot + LAG)
        if slot in splits:
            split_range(*splits[slot])
        if slot in BATCHES:
            b = list(BATCHES).index(slot)
            if ("y", 7) in BATCHES[slot]:
                y_wait(7)
            stage_one(b)
            if b:
                stage_three(b - 1)
            stage_two(b)

    def owner_sum(total, first, end):
        for n in range(first, end):
            if n:
                owner_copies[n].wait_recv()
            total = total + crow[n]
        return total

    total = owner_sum(jnp.zeros((16, 128), jnp.float32), 0, 2 * NB - 4)
    stage_three(NB - 1)
    total = owner_sum(total, 2 * NB - 4, 2 * NB)
    turned = pltpu.roll(total, 64, 1)
    ladder = jnp.concatenate([total, turned[0:8]], axis=0)
    out[...] = (ladder / den[...])[:, :MINE]

    for copy in ycopies + list(ring.values()) + core_copies + sum(x_copies, []) + list(owner_copies.values()):
        copy.wait_send()


def per_device(amplitudes, integrals, pair_index, occ_energy, virt_energy):
    dma = pltpu.SemaphoreType.DMA

    def f32(*shape):
        return pltpu.VMEM(shape, jnp.float32)

    def bf16(*shape):
        return pltpu.VMEM(shape, jnp.bfloat16)

    return pl.pallas_call(
        kernel,
        out_shape=jax.ShapeDtypeStruct((ROWS, MINE), jnp.float32),
        in_specs=[pl.BlockSpec(memory_space=pl.ANY)] * 2 + [pl.BlockSpec(memory_space=pltpu.SMEM)] * 3,
        out_specs=pl.BlockSpec(memory_space=pltpu.VMEM),
        scratch_shapes=[
            f32(ROWS, COLS), f32(WINDOW, EACH), bf16(4, WIDE, 256), bf16(4, WIDE, 256),
            f32(16, 8, SENT), f32(8, 8, SENT), f32(16, 8, SENT), f32(16, 8, SENT),
            bf16(96, WIDE), f32(NB, 2, 48, 512), f32(NB, 48, 512), f32(NB, 8, ROWS, 128), f32(NB, 7, ROWS, 128),
            f32(2 * NB, 16, 128), f32(2 * NB, 16, 128), f32(ROWS, 128),
            dma, dma, dma((8,)), dma((8,)), dma((16,)), dma((16,)), dma((16,)), dma((16,)),
            dma((NB,)), dma((NB,)), dma((NB, 7)), dma((NB, 7)), dma((2 * NB,)), dma((2 * NB,)),
        ],
        compiler_params=pltpu.CompilerParams(
            collective_id=0, has_side_effects=True, vmem_limit_bytes=60 * 2**20
        ),
        cost_estimate=pl.CostEstimate(flops=4_700_000_000, bytes_accessed=12_000_000, transcendentals=0),
        name="ladder",
    )(amplitudes, integrals, pair_index, occ_energy, virt_energy)


def solution(mesh):
    return jax.shard_map(
        per_device,
        mesh=mesh,
        in_specs=(P("cd", "ab"), P(None, ("ab", "cd")), P("cd"), P(), P()),
        out_specs=P("cd", "ab"),
        check_vma=False,
    )
```

time: 343 us -> 114 us (0.33)
  waiting for transfers between devices: 203 us -> 0 us
  Pallas kernels: 0 us -> 112 us
  blocking collectives: 97.7 us -> 0 us
  between operations: 14.2 us -> 0.01 us
  matrix products: 14 us -> 0 us
  local copies, waits for them, and re-layouts: 11.2 us -> 1.31 us
    unnamed x4 -> x0, waiting for transfers between devices: 203 us -> none
    pallas_call x0 -> x1, Pallas kernels: none -> 112 us  [per_device(): pl.pallas_call(kernel, out_shape=jax.ShapeDtypeStruct((ROWS, MINE), jnp.f...]
    all_to_all x1 -> x0, blocking collectives: 97.7 us -> none  [per_device(): lax.all_to_all(blocks, 'cd', split_axis=1, concat_axis=0, tiled=True)]
    dot_general x1 -> x0, matrix products: 14 us -> none  [per_device(): lax.dot_general(received, integrals, (((1,), (1,)), ((), ())), precision=...]
    reshape x2 -> x0, local copies, waits for them, and re-layouts: 10.5 us -> none  [per_device(): blocks = amplitudes.reshape(local_rows, pieces, width_each)]
  transfers between devices with their start and end apart: 2 -> 0, of which waited for: 2 -> 0; matrix products, arithmetic and copies ran while one was open for 0% -> 0% of each run, Pallas kernels for 0% -> 0%
where the time goes in v1:
time: 114 us; the launch traced here: 113 us
  Pallas kernels  112 us (98%)
  local copies, waits for them, and re-layouts  1.31 us (1%)
    pallas_call x1, Pallas kernels, per_device(): pl.pallas_call(kernel, out_shape=jax.ShapeDtypeStruct((ROWS, MINE), jnp.f...  112 us

profile of v1, /device:TPU:1, one launch (start us, length us, event | category | flops | bytes accessed | tf_op | source)
XLA Modules:
  0.0 113.5 jit_solution(2007996153649243388)
XLA Ops:
  0.0 112.1 %ladder.1 = f32[24,50]{1,0:T(8,128)} custom-call(f32[24,40000]{1,0:T(8,128)} %amp.1, f32[800,2500]{1,0:T(8,128)} %integrals.1, s32[24]{0:T(128)} %pair_ref.1, f32[100]{0:T(128)} %occ_ref.1, f32[800]{0:T(1024)} %virt_ref.1), custom_call_target="tpu_custom_call" | custom-call | flops 4700000256 | bytes 12000000 | tf_op jit(solution)/shard_map/ladder/pallas_call | solution.py:357
  112.2 1.3 %copy.7 = f32[24,50]{1,0:T(8,128)} copy(f32[24,50]{1,0:T(8,128)} %ladder.1) | data formatting | bytes 9600

commit v2 on v1

v2 whole, which is shorter than its diff:
```python
import functools

import jax
import jax.numpy as jnp
from jax import lax
from jax.experimental import pallas as pl
from jax.experimental.pallas import tpu as pltpu
from jax.sharding import PartitionSpec as P

NOCC = 100
NV = 800
MESH = pl.DeviceIdType.MESH

ROWS = 24
EACH = 2500
WIDE = 2560
TILES = WIDE // 128
FULL = EACH // 128
REST = EACH - FULL * 128
SENT = (3 * FULL + 2) * 128
HALF_TILES = 10
HALF = HALF_TILES * 3 * 128
COLS = 40000
WINDOW = 800
MINE = 50
LAG = 3

SEQUENCE = (
    ("A4", "half"), ("A3", "all"), ("A2", "all"), ("A4", "half"), ("A3", "all"), ("B4", "half"), ("A4", "half"),
    ("A3", "all"), ("B4", "half"), ("A4", "half"), ("B3", "all"), ("B4", "half"), ("B2", "all"), ("B3", "all"),
    ("B4", "half"), ("B2", "all"), ("B3", "all"), ("A2", "all"), ("B1", "all"), ("A1", "all"),
)
SLOTS = len(SEQUENCE)
CROSS = ("B4", "B3p", "B3m", "B2p", "B2m", "B1p", "B1m", "B0")
OWN = ("A4", "A3p", "A3m", "A2p", "A2m", "A1p", "A1m", "A0")
PLACE = {name: k for k, name in enumerate(CROSS + OWN)}
BATCHES = {
    7: ("A3p", "A3m"),
    11: ("A0", "B0"),
    14: ("A4", "B4"),
    15: ("B2p", "B2m"),
    16: ("B3p", "B3m"),
    17: ("A2p", "A2m"),
    18: ("B1p", "B1m"),
    19: ("A1p", "A1m"),
}
NB = len(BATCHES)
PAIRS = tuple(BATCHES.values())
INBOX = {name: k for k, name in enumerate(CROSS + OWN[:-1])}
SEND_ON = {
    1: ("B0",), 2: ("B4",), 3: ("B2p", "B2m", "A4"), 4: ("B3p", "B3m"), 5: ("A2p", "A2m", "A3p", "A3m"), 6: ("B1p", "B1m"),
}


def kernel(
    amp, integrals, pair, occ, virt, out,
    amp_v, int_v, vhi, vlo, pack, ybuf, pbuf, mbuf, lhs, part, crecv, xs, xrecv, sums, outbox, inbox, den, pair_ref, occ_ref, virt_ref,
    amp_sem, int_sem, table_sem, ysend, yrecv, psend, precv, msend, mrecv, c_s, c_r, x_s, x_r, d_s, d_r,
):
    ab, cd = lax.axis_index("ab"), lax.axis_index("cd")
    core, x, yh = ab % 2, (ab // 2) % 4, ab // 8
    yl, z = cd // 8, cd % 8

    def on_ab(h, xx, c):
        return ((h * 4 + xx) * 2 + c, cd)

    def on_cd(y, zz):
        return (ab, y * 8 + zz)

    amp_copy = pltpu.make_async_copy(amp, amp_v, amp_sem)
    int_copy = pltpu.make_async_copy(integrals, int_v, int_sem)
    amp_copy.start()

    partner_core = on_ab(yh, x, 1 - core)
    x_order = (6, 5, 7, 2, 4, 1, 3)
    partners_x = [on_ab((yh + k // 4) % 2, (x + k) % 4, core) for k in x_order]
    partner_yl = on_cd(1 - yl, z)
    up, down = on_cd(yl, (z + 1) % 8), on_cd(yl, (z + 7) % 8)
    greeted = [up, down, partner_yl, partner_core] + partners_x
    barrier = pltpu.get_barrier_semaphore()
    for device in greeted:
        pl.semaphore_signal(barrier, inc=1, device_id=device, device_id_type=MESH)

    lane = lax.broadcasted_iota(jnp.int32, (ROWS, 128), 1)
    lane8 = lax.broadcasted_iota(jnp.int32, (8, 128), 1)

    def owner_piece(k):
        name = (CROSS + OWN)[k]
        step = int(name[1]) if name[-1] != "m" else 8 - int(name[1])
        column = yl if name[0] == "A" else 1 - yl
        return column * 8 + (z + step) % 8

    def pack_block(k):
        piece = owner_piece(k)
        begin = piece * EACH
        tile = begin // 128
        off = begin - tile * 128
        turn = lax.rem(128 - off, 128)
        tail = jnp.concatenate(
            [amp_v[:, COLS - 64 : COLS], jnp.zeros((ROWS, 64), jnp.float32)], axis=1
        )
        keep = lane < 128 - off

        def rolled(j):
            if j < TILES:
                block = amp_v[:, pl.ds(pl.multiple_of((tile + j) * 128, 128), 128)]
            else:
                at = jnp.minimum(tile + TILES, COLS // 128 - 1)
                block = amp_v[:, pl.ds(pl.multiple_of(at * 128, 128), 128)]
                block = jnp.where(piece == 15, tail, block)
            return pltpu.roll(block, turn, 1)

        now = rolled(0)
        for j in range(FULL):
            later = rolled(j + 1)
            value = jnp.where(keep, now, later)
            for r in range(3):
                pack[k, :, (3 * j + r) * 128 : (3 * j + r + 1) * 128] = value[r * 8 : r * 8 + 8]
            now = later
        value = jnp.where(keep, now, rolled(FULL + 1))
        one, two, three = value[0:8], value[8:16], value[16:24]
        pack[k, :, 3 * FULL * 128 : (3 * FULL + 1) * 128] = jnp.where(lane8 < 64, one, pltpu.roll(two, 64, 1))
        over = REST - 64
        rests = jnp.where(lane8 < REST + over, pltpu.roll(one, over, 1), pltpu.roll(two, 2 * over, 1))
        rests = jnp.where(lane8 < REST + 2 * over, rests, 0.0)
        pack[k, :, (3 * FULL + 1) * 128 : SENT] = jnp.where(lane8 < REST, three, rests)

    def last_tile(tile_of):
        first, second = tile_of(3 * FULL), tile_of(3 * FULL + 1)
        over = REST - 64
        one = jnp.where(lane8 < 64, first, pltpu.roll(second, 128 - over, 1))
        two = jnp.where(lane8 < 64, pltpu.roll(first, 64, 1), pltpu.roll(second, 128 - 2 * over, 1))
        return [jnp.where(lane8 < REST, rest, 0.0) for rest in (one, two, second)]

    def remote(src, dst, send, recv, device):
        return pltpu.make_async_remote_copy(
            src_ref=src, dst_ref=dst, send_sem=send, recv_sem=recv, device_id=device, device_id_type=MESH
        )

    ycopies = [remote(pack.at[k], ybuf.at[k], ysend.at[k], yrecv.at[k], partner_yl) for k in range(8)]
    state = {"y_started": 0, "y_waited": 0}
    packed = set()

    def ensure_pack(k):
        if k not in packed:
            packed.add(k)
            pack_block(k)

    def y_start():
        k = state["y_started"]
        if k < 8:
            ensure_pack(k)
            ycopies[k].start()
            state["y_started"] = k + 1

    def y_wait(k):
        while state["y_waited"] <= k:
            ycopies[state["y_waited"]].wait_recv()
            state["y_waited"] += 1
            y_start()

    ring, needs, arrived = {}, {}, {}
    for way, device, buf, send, recv in (("p", up, pbuf, psend, precv), ("m", down, mbuf, msend, mrecv)):
        last = {}
        for slot, (name, size) in enumerate(SEQUENCE):
            if size == "all":
                columns = slice(0, SENT)
            elif size == "first" or (size == "half" and way == "p"):
                columns = slice(0, HALF)
            else:
                columns = slice(HALF, SENT)
            full = name if name[1] == "4" else name + way
            if name in last and size != "second":
                src, need = buf.at[last[name]], None
            else:
                k = PLACE[full]
                need = ("y", k) if k < 8 else ("pack", k)
                src = (ybuf if k < 8 else pack).at[k]
            last[name] = slot
            arrived[full, columns.start] = (way, slot)
            ring[way, slot] = remote(
                src.at[:, columns], buf.at[slot].at[:, columns], send.at[slot], recv.at[slot], device
            )
            needs[way, slot] = need

    def ring_start(way, slot):
        if slot >= SLOTS:
            return
        need = needs[way, slot]
        if need is not None and need[0] == "pack":
            ensure_pack(need[1])
        elif need is not None:
            y_wait(need[1])
        ring[way, slot].start()

    def split_columns(at, width):
        for place in range(0, 1024, 128):
            pieces = []
            for h in (0, 1):
                g = (h * 4 + place // 128 % 4) * 2 + place // 512
                value = int_v[g * MINE : (g + 1) * MINE, pl.ds(at, width)]
                if width < 128:
                    value = jnp.concatenate([value, jnp.zeros((MINE, 128 - width), jnp.float32)], axis=1)
                pieces += [value, jnp.zeros((64 - MINE, 128), jnp.float32)]
            value = jnp.concatenate(pieces, axis=0).T
            high = value.astype(jnp.bfloat16)
            low = (value - high.astype(jnp.float32)).astype(jnp.bfloat16)
            vhi[place // 256, pl.ds(at, 128), place % 256 : place % 256 + 128] = high
            vlo[place // 256, pl.ds(at, 128), place % 256 : place % 256 + 128] = low

    def split_range(first, end):
        def body(j, carry):
            split_columns(pl.multiple_of(j * 128, 128), 128)
            return carry

        lax.fori_loop(first, end, body, 0)

    def tile_reader(name):
        def tile_of(t):
            columns = slice(t * 128, t * 128 + 128)
            if name == "A0":
                return pack[PLACE[name], :, columns]
            if name == "B0":
                return ybuf[PLACE[name], :, columns]
            start = HALF if t * 128 >= HALF and (name, HALF) in arrived else 0
            way, slot = arrived[name, start]
            return (pbuf if way == "p" else mbuf)[slot, :, columns]

        return tile_of

    core_copies = [remote(part.at[b, 1 - core], crecv.at[b], c_s.at[b], c_r.at[b], partner_core) for b in range(NB)]
    x_copies = [
        [
            remote(
                xs.at[b, (yh + k // 4) % 2 * 4 + (x + k) % 4],
                xrecv.at[b, i], x_s.at[b, i], x_r.at[b, i], partners_x[i],
            )
            for i, k in enumerate(x_order)
        ]
        for b in range(NB)
    ]
    owner_copies = {}
    for name, k in INBOX.items():
        step = int(name[1]) if name[-1] == "m" else (8 - int(name[1])) % 8
        device = partner_yl if name[0] == "B" else on_cd(yl, (z + step) % 8)
        owner_copies[name] = remote(outbox.at[k], inbox.at[k], d_s.at[k], d_r.at[k], device)

    def multiply(b, first, end):
        one, two = (tile_reader(name) for name in PAIRS[b])
        for j in range(first, end):
            if j < FULL:
                pieces = [tile_of(3 * j + r) for tile_of in (one, two) for r in range(3)]
            else:
                pieces = last_tile(one) + last_tile(two)
            value = jnp.concatenate(pieces, axis=0)
            high = value.astype(jnp.bfloat16)
            lhs[0:48, j * 128 : (j + 1) * 128] = high
            lhs[48:96, j * 128 : (j + 1) * 128] = (value - high.astype(jnp.float32)).astype(jnp.bfloat16)
        dims = (((1,), (0,)), ((), ()))
        depth = slice(first * 128, end * 128)
        for k in range(4):
            half = 1 - core if k < 2 else core
            n = half * 2 + k % 2
            main = lax.dot_general(lhs[:, depth], vhi[n, depth], dims, preferred_element_type=jnp.float32)
            rest = lax.dot_general(lhs[0:48, depth], vlo[n, depth], dims, preferred_element_type=jnp.float32)
            total = main[0:48] + main[48:96] + rest
            columns = slice((k % 2) * 256, (k % 2) * 256 + 256)
            if first:
                total = total + part[b, half, :, columns]
            part[b, half, :, columns] = total
            if k == 1 and end == TILES:
                core_copies[b].start()

    def stage_two(b):
        core_copies[b].wait_recv()
        for k in range(4):
            value = part[b, core, :, k * 128 : (k + 1) * 128] + crecv[b, :, k * 128 : (k + 1) * 128]
            turned = pltpu.roll(value, 64, 1)
            xs[b, k] = jnp.where(lane < 64, value[0:ROWS], turned[ROWS:])
            xs[b, 4 + k] = jnp.where(lane < 64, turned[0:ROWS], value[ROWS:])
        for copy in x_copies[b]:
            copy.start()

    def stage_three(b):
        value = xs[b, yh * 4 + x]
        for k, copy in enumerate(x_copies[b]):
            copy.wait_recv()
            value = value + xrecv[b, k]
        turned = pltpu.roll(value, 64, 1)
        for i in (0, 1):
            low, high = (value, turned) if i == 0 else (turned, value)
            high = jnp.concatenate([high[16:24], jnp.zeros((8, 128), jnp.float32)], axis=0)
            sums[2 * b + i] = jnp.where(lane[0:16] < 64, low[0:16], high)

    def sum_of(name, inputs):
        b = [name in pair for pair in PAIRS].index(True)
        value = sums[2 * b + PAIRS[b].index(name)]
        for key in inputs:
            owner_copies[key].wait_recv()
            value = value + inbox[INBOX[key]]
        return value

    def send_on(name):
        outbox[INBOX[name]] = sum_of(name, ("B" + name[1:],) if name[0] == "A" else ())
        owner_copies[name].start()

    pl.semaphore_wait(barrier, len(greeted))
    amp_copy.wait()

    y_start()
    for slot in range(LAG):
        ring_start("p", slot)
        ring_start("m", slot)
    y_start()
    y_start()
    for k in range(16):
        ensure_pack(k)

    int_copy.start()
    tables = [
        pltpu.make_async_copy(source, table, table_sem.at[k])
        for k, (source, table) in enumerate(((pair, pair_ref), (occ, occ_ref), (virt, virt_ref)))
    ]
    for copy in tables:
        copy.start()
    for copy in tables:
        copy.wait()

    row24 = lax.broadcasted_iota(jnp.int32, (ROWS, 128), 0)
    occ_pair = jnp.zeros((ROWS, 128), jnp.float32)
    for r in range(ROWS):
        both = pair_ref[r]
        occ_pair = jnp.where(row24 == r, occ_ref[both // NOCC] + occ_ref[both % NOCC], occ_pair)
    virt_pair = jnp.zeros((ROWS, 128), jnp.float32)
    for c in range(MINE):
        row = ab * MINE + c
        virt_pair = jnp.where(lane == c, virt_ref[row // NV] + virt_ref[row % NV], virt_pair)
    den[...] = occ_pair - virt_pair

    int_copy.wait()
    split_columns(FULL * 128, REST)
    splits = {0: (0, 6), 1: (6, 12), 2: (12, 19)}

    for slot in range(SLOTS):
        for way in ("p", "m"):
            ring[way, slot].wait_recv()
            ring_start(way, slot + LAG)
        if slot in splits:
            split_range(*splits[slot])
        if slot == SLOTS - 1:
            multiply(NB - 1, 0, TILES)
            stage_three(NB - 2)
            for name in SEND_ON[NB - 2]:
                send_on(name)
            stage_two(NB - 1)
        elif slot in BATCHES:
            b = list(BATCHES).index(slot)
            if "B0" in BATCHES[slot]:
                y_wait(7)
            multiply(b, 0, TILES)
            if b:
                stage_three(b - 1)
                for name in SEND_ON.get(b - 1, ()):
                    send_on(name)
            stage_two(b)

    stage_three(NB - 1)
    send_on("A1p")
    send_on("A1m")
    total = sum_of("A0", ("B0",) + OWN[:-1])
    turned = pltpu.roll(total, 64, 1)
    ladder = jnp.concatenate([total, turned[0:8]], axis=0)
    out[...] = (ladder / den[...])[:, :MINE]

    for copy in ycopies + list(ring.values()) + core_copies + sum(x_copies, []) + list(owner_copies.values()):
        copy.wait_send()


def per_device(amplitudes, integrals, pair_index, occ_energy, virt_energy):
    dma = pltpu.SemaphoreType.DMA

    def f32(*shape):
        return pltpu.VMEM(shape, jnp.float32)

    def bf16(*shape):
        return pltpu.VMEM(shape, jnp.bfloat16)

    return pl.pallas_call(
        kernel,
        out_shape=jax.ShapeDtypeStruct((ROWS, MINE), jnp.float32),
        in_specs=[pl.BlockSpec(memory_space=pl.ANY)] * 5,
        out_specs=pl.BlockSpec(memory_space=pltpu.VMEM),
        scratch_shapes=[
            f32(ROWS, COLS), f32(WINDOW, EACH), bf16(4, WIDE, 256), bf16(4, WIDE, 256),
            f32(16, 8, SENT), f32(8, 8, SENT), f32(SLOTS, 8, SENT), f32(SLOTS, 8, SENT),
            bf16(96, WIDE), f32(NB, 2, 48, 512), f32(NB, 48, 512), f32(NB, 8, ROWS, 128), f32(NB, 7, ROWS, 128),
            f32(2 * NB, 16, 128), f32(len(INBOX), 16, 128), f32(len(INBOX), 16, 128), f32(ROWS, 128),
            pltpu.SMEM((ROWS,), jnp.int32), pltpu.SMEM((NOCC,), jnp.float32), pltpu.SMEM((NV,), jnp.float32),
            dma, dma, dma((3,)), dma((8,)), dma((8,)), dma((SLOTS,)), dma((SLOTS,)), dma((SLOTS,)), dma((SLOTS,)),
            dma((NB,)), dma((NB,)), dma((NB, 7)), dma((NB, 7)), dma((len(INBOX),)), dma((len(INBOX),)),
        ],
        compiler_params=pltpu.CompilerParams(
            collective_id=0, has_side_effects=True, vmem_limit_bytes=60 * 2**20
        ),
        cost_estimate=pl.CostEstimate(flops=4_700_000_000, bytes_accessed=12_000_000, transcendentals=0),
        name="ladder",
    )(amplitudes, integrals, pair_index, occ_energy, virt_energy)


def solution(mesh):
    return jax.shard_map(
        per_device,
        mesh=mesh,
        in_specs=(P("cd", "ab"), P(None, ("ab", "cd")), P("cd"), P(), P()),
        out_specs=P("cd", "ab"),
        check_vma=False,
    )
```

time: 114 us -> 112 us (0.982)
    pallas_call x1, Pallas kernels: 112 us -> 111 us  [per_device(): pl.pallas_call(kernel, out_shape=jax.ShapeDtypeStruct((ROWS, MINE), jnp.f...]
where the time goes in v2:
time: 112 us
  Pallas kernels  111 us (99%)
  local copies, waits for them, and re-layouts  1.31 us (1%)
    pallas_call x1, Pallas kernels, per_device(): pl.pallas_call(kernel, out_shape=jax.ShapeDtypeStruct((ROWS, MINE), jnp.f...  111 us

profile of v2, /device:TPU:1, one launch (start us, length us, event | category | flops | bytes accessed | tf_op | source)
XLA Modules:
  0.0 112.1 jit_solution(4070246329024218761)
XLA Ops:
  0.0 110.8 %ladder.1 = f32[24,50]{1,0:T(8,128)} custom-call(f32[24,40000]{1,0:T(8,128)} %amp.1, f32[800,2500]{1,0:T(8,128)} %integrals.1, s32[24]{0:T(128)} %pair.1, f32[100]{0:T(128)} %occ.1, f32[800]{0:T(1024)} %virt.1), custom_call_target="tpu_custom_call" | custom-call | flops 4700000256 | bytes 12000000 | tf_op jit(solution)/shard_map/ladder/pallas_call | solution.py:388
  110.8 1.3 %copy.7 = f32[24,50]{1,0:T(8,128)} copy(f32[24,50]{1,0:T(8,128)} %ladder.1) | data formatting | bytes 9600

commit v3 on v2

--- a/solution.py
+++ b/solution.py
@@ -18,8 +18,7 @@
 FULL = EACH // 128
 REST = EACH - FULL * 128
 SENT = (3 * FULL + 2) * 128
-HALF_TILES = 10
-HALF = HALF_TILES * 3 * 128
+HALF = 10 * 3 * 128
 COLS = 40000
 WINDOW = 800
 MINE = 50
@@ -165,12 +164,12 @@
         for slot, (name, size) in enumerate(SEQUENCE):
             if size == "all":
                 columns = slice(0, SENT)
-            elif size == "first" or (size == "half" and way == "p"):
+            elif way == "p":
                 columns = slice(0, HALF)
             else:
                 columns = slice(HALF, SENT)
             full = name if name[1] == "4" else name + way
-            if name in last and size != "second":
+            if name in last:
                 src, need = buf.at[last[name]], None
             else:
                 k = PLACE[full]
@@ -303,16 +302,16 @@
     def send_on(name):
         outbox[INBOX[name]] = sum_of(name, ("B" + name[1:],) if name[0] == "A" else ())
         owner_copies[name].start()
-
+        sent.append(name)
+
+    amp_copy.wait()
+    ensure_pack(PLACE["A4"])
     pl.semaphore_wait(barrier, len(greeted))
-    amp_copy.wait()
-
-    y_start()
+
     for slot in range(LAG):
         ring_start("p", slot)
         ring_start("m", slot)
-    y_start()
-    y_start()
+        y_start()
     for k in range(16):
         ensure_pack(k)
 
@@ -341,39 +340,61 @@
     split_columns(FULL * 128, REST)
     splits = {0: (0, 6), 1: (6, 12), 2: (12, 19)}
 
+    waits = {"ring": 0, "batch": 0, "cross": 0}
+    sent = []
+
+    def settle(slot, batch):
+        while waits["ring"] <= slot:
+            for way in ("p", "m"):
+                ring[way, waits["ring"]].wait_send()
+            waits["ring"] += 1
+        while waits["cross"] < state["y_waited"] - 1:
+            ycopies[waits["cross"]].wait_send()
+            waits["cross"] += 1
+        while waits["batch"] <= batch:
+            for copy in [core_copies[waits["batch"]]] + x_copies[waits["batch"]]:
+                copy.wait_send()
+            waits["batch"] += 1
+
     for slot in range(SLOTS):
         for way in ("p", "m"):
             ring[way, slot].wait_recv()
             ring_start(way, slot + LAG)
         if slot in splits:
             split_range(*splits[slot])
-        if slot == SLOTS - 1:
-            multiply(NB - 1, 0, TILES)
-            stage_three(NB - 2)
-            for name in SEND_ON[NB - 2]:
-                send_on(name)
-            stage_two(NB - 1)
-        elif slot in BATCHES:
+        if slot in BATCHES:
             b = list(BATCHES).index(slot)
             if "B0" in BATCHES[slot]:
                 y_wait(7)
             multiply(b, 0, TILES)
+            if b == NB - 1:
+                stage_two(b)
             if b:
                 stage_three(b - 1)
                 for name in SEND_ON.get(b - 1, ()):
                     send_on(name)
-            stage_two(b)
-
+            if b < NB - 1:
+                stage_two(b)
+                settle(slot - 3, b - 2)
+        else:
+            settle(slot - 3, -1)
+
+    for name in sent[:-2]:
+        owner_copies[name].wait_send()
+    settle(SLOTS - 4, NB - 3)
+    total = sum_of("A0", ("B0",) + OWN[:-3])
     stage_three(NB - 1)
     send_on("A1p")
     send_on("A1m")
-    total = sum_of("A0", ("B0",) + OWN[:-1])
+    settle(SLOTS - 1, NB - 1)
+    for copy in ycopies[waits["cross"] :] + [owner_copies[name] for name in sent[-4:]]:
+        copy.wait_send()
+    for name in ("A1p", "A1m"):
+        owner_copies[name].wait_recv()
+        total = total + inbox[INBOX[name]]
     turned = pltpu.roll(total, 64, 1)
     ladder = jnp.concatenate([total, turned[0:8]], axis=0)
     out[...] = (ladder / den[...])[:, :MINE]
-
-    for copy in ycopies + list(ring.values()) + core_copies + sum(x_copies, []) + list(owner_copies.values()):
-        copy.wait_send()
 
 
 def per_device(amplitudes, integrals, pair_index, occ_energy, virt_energy):

time: 112 us -> 112 us (level)
  no operation moved by 1% of the time
where the time goes in v3:
time: 112 us
  Pallas kernels  110 us (98%)
  local copies, waits for them, and re-layouts  1.31 us (1%)
    pallas_call x1, Pallas kernels, per_device(): pl.pallas_call(kernel, out_shape=jax.ShapeDtypeStruct((ROWS, MINE), jnp.f...  110 us

profile of v3, /device:TPU:1, one launch (start us, length us, event | category | flops | bytes accessed | tf_op | source)
XLA Modules:
  0.0 111.7 jit_solution(957341120852230739)
XLA Ops:
  0.0 110.4 %ladder.1 = f32[24,50]{1,0:T(8,128)} custom-call(f32[24,40000]{1,0:T(8,128)} %amp.1, f32[800,2500]{1,0:T(8,128)} %integrals.1, s32[24]{0:T(128)} %pair.1, f32[100]{0:T(128)} %occ.1, f32[800]{0:T(1024)} %virt.1), custom_call_target="tpu_custom_call" | custom-call | flops 4700000256 | bytes 12000000 | tf_op jit(solution)/shard_map/ladder/pallas_call | solution.py:409
  110.4 1.3 %copy.7 = f32[24,50]{1,0:T(8,128)} copy(f32[24,50]{1,0:T(8,128)} %ladder.1) | data formatting | bytes 9600

commit v4 on v3

--- a/solution.py
+++ b/solution.py
@@ -22,7 +22,7 @@
 COLS = 40000
 WINDOW = 800
 MINE = 50
-LAG = 3
+LAG = 2
 
 SEQUENCE = (
     ("A4", "half"), ("A3", "all"), ("A2", "all"), ("A4", "half"), ("A3", "all"), ("B4", "half"), ("A4", "half"),

time: 112 us -> 123 us (1.098)
  Pallas kernels: 110 us -> 122 us
    pallas_call x1, Pallas kernels: 110 us -> 122 us  [per_device(): pl.pallas_call(kernel, out_shape=jax.ShapeDtypeStruct((ROWS, MINE), jnp.f...]
where the time goes in v4:
time: 123 us
  Pallas kernels  122 us (99%)
  local copies, waits for them, and re-layouts  1.31 us (1%)
    pallas_call x1, Pallas kernels, per_device(): pl.pallas_call(kernel, out_shape=jax.ShapeDtypeStruct((ROWS, MINE), jnp.f...  122 us

profile of v4, /device:TPU:1, one launch (start us, length us, event | category | flops | bytes accessed | tf_op | source)
XLA Modules:
  0.0 123.0 jit_solution(14803032971726089055)
XLA Ops:
  0.0 121.7 %ladder.1 = f32[24,50]{1,0:T(8,128)} custom-call(f32[24,40000]{1,0:T(8,128)} %amp.1, f32[800,2500]{1,0:T(8,128)} %integrals.1, s32[24]{0:T(128)} %pair.1, f32[100]{0:T(128)} %occ.1, f32[800]{0:T(1024)} %virt.1), custom_call_target="tpu_custom_call" | custom-call | flops 4700000256 | bytes 12000000 | tf_op jit(solution)/shard_map/ladder/pallas_call | solution.py:409
  121.7 1.3 %copy.7 = f32[24,50]{1,0:T(8,128)} copy(f32[24,50]{1,0:T(8,128)} %ladder.1) | data formatting | bytes 9600
